TPU v7x, 32 devices: a whole 2x2x4 slice. The times are simulated.
32 devices in a mesh: dp: 4 (over z), seq: 8 (over y, x, core).
Axes of the slice: x: 2, y: 2, z: 4, core: 2. Of those that a mesh axis runs over, the one named last changes fastest.
Arguments:
- tokens: bfloat16 [4, 8192, 768], P('dp', 'seq'), may hold values from -6 to 6
- cotangent: bfloat16 [4, 8192, 768], P('dp', 'seq'), may hold values from -6 to 6
- first_gain: float32 [768], replicated, may hold values from 0.25 to 1.75
- first_shift: float32 [768], replicated, may hold values from -1.75 to 1.75
- joint_weight: bfloat16 [768, 2304], replicated, may hold values from -0.21875 to 0.21875
- query_bias: float32 [768], replicated, may hold values from -3 to 3
- value_bias: float32 [768], replicated, may hold values from -3 to 3
- score_weight: bfloat16 [768, 12], replicated, may hold values from -0.3125 to 0.3125
- out_weight: bfloat16 [768, 768], replicated, may hold values from -1.75 to 1.75
- out_bias: float32 [768], replicated, may hold values from -3 to 3
- second_gain: float32 [768], replicated, may hold values from 0.25 to 1.75
- second_shift: float32 [768], replicated, may hold values from -1.75 to 1.75
- expand_weight: bfloat16 [768, 3072], replicated, may hold values from -0.21875 to 0.21875
- expand_bias: float32 [3072], replicated, may hold values from -3 to 3
- reduce_weight: bfloat16 [3072, 768], replicated, may hold values from -0.109375 to 0.109375
- reduce_bias: float32 [768], replicated, may hold values from -3 to 3
- picks: int32 [4, 8, 8, 8], P('dp', 'seq'), may hold values from 0 to 1023
- quota: int32 [4, 8, 8], P('dp', 'seq'), may hold values from 0 to 8, as said below
Outputs:
- layer_out: bfloat16 [4, 8192, 768], P('dp', 'seq')
- token_grad: float32 [4, 8192, 768], P('dp', 'seq')
- first_gain_grad: float32 [768], replicated
- first_shift_grad: float32 [768], replicated
- joint_weight_grad: float32 [768, 2304], replicated
- query_bias_grad: float32 [768], replicated
- value_bias_grad: float32 [768], replicated
- score_weight_grad: float32 [768, 12], replicated
- out_weight_grad: float32 [768, 768], replicated
- out_bias_grad: float32 [768], replicated
- second_gain_grad: float32 [768], replicated
- second_shift_grad: float32 [768], replicated
- expand_weight_grad: float32 [768, 3072], replicated
- expand_bias_grad: float32 [3072], replicated
- reduce_weight_grad: float32 [3072, 768], replicated
- reduce_bias_grad: float32 [768], replicated
Inputs may be any that keep to these rules, and one draw needn't show every extreme that they name: quota[s, d] is zero where s > d; the last query block takes 8 keys from every block. `picks`: only entries with c < quota[s, d] are read.
All inputs are finite; a program needn't handle non-finite values.
Results may differ from a plain program's by a relative error of at most 0.011.
Values may be sent and summed in bfloat16 or wider, within the bound.
No kernel may reach another device: no remote copies, remote signals or barrier semaphores. Data moves between devices by JAX's collectives and lax.ppermute only.
A program may use at most 192 MiB of HBM per device.

v0:
```python
import math
import jax
import jax.numpy as jnp
from jax import lax
from jax.sharding import PartitionSpec as P

WIN = 64
PICK = 8
epsilon = 1e-05
very_low = -1e30


def passed_along(value, axis, steps):
    count = lax.axis_size(axis)
    leading, last = (max(0, -steps), min(count, count - steps))
    return lax.ppermute(value, axis, [(source, source + steps) for source in range(leading, last)])


def layer_norm_parts(values, gain, shift):
    average = jnp.mean(values, axis=-1, keepdims=True)
    centred = values - average
    variance = jnp.mean(centred * centred, axis=-1, keepdims=True)
    inverse = lax.rsqrt(variance + epsilon)
    unit = centred * inverse
    return (unit * gain + shift, unit, inverse)


def layer_norm_back(grad_out, unit, inverse, gain):
    grad_unit = grad_out * gain
    mean_grad = jnp.mean(grad_unit, axis=-1, keepdims=True)
    mean_cross = jnp.mean(grad_unit * unit, axis=-1, keepdims=True)
    grad_in = (grad_unit - mean_grad - unit * mean_cross) * inverse
    return (grad_in, jnp.sum(grad_out * unit, axis=0), jnp.sum(grad_out, axis=0))


def gelu_tanh(values):
    return (
        0.5
        * values
        * (1.0 + jnp.tanh(0.7978845608028654 * (values + 0.044715 * values * values * values)))
    )


def cross(left, right):
    return lax.dot_general(
        left, right, (((0,), (0,)), ((), ())), preferred_element_type=jnp.float32
    )


def times_transposed(left, right):
    return lax.dot_general(
        left, right, (((1,), (1,)), ((), ())), preferred_element_type=jnp.float32
    )


def pair_tiles(values, tiles, window):
    shaped = values.reshape((tiles + 1, window) + values.shape[1:])
    return jnp.concatenate([shaped[:-1], shaped[1:]], axis=1)


def arrange(rim, packed, far_packed, far_pos, place, heads, head_size):
    rows = packed.shape[0]
    width = heads * head_size
    tiles = rows // WIN
    near = pair_tiles(jnp.concatenate([rim, packed], axis=0), tiles, WIN)
    near_key = near[..., :width].reshape(tiles, 2 * WIN, heads, head_size)
    near_value = near[..., width : 2 * width].reshape(tiles, 2 * WIN, heads, head_size)
    near_score = near[..., 2 * width :].astype(jnp.float32)
    far_flat = far_packed.reshape(-1, far_packed.shape[-1])
    far_key = far_flat[:, :width].reshape(-1, heads, head_size)
    far_value = far_flat[:, width : 2 * width].reshape(-1, heads, head_size)
    far_score = far_flat[:, 2 * width :].astype(jnp.float32)
    start = place * rows
    ext_pos = start - WIN + jnp.arange(rows + WIN, dtype=jnp.int32)
    near_pos = pair_tiles(ext_pos, tiles, WIN)
    query_pos = (start + jnp.arange(rows, dtype=jnp.int32)).reshape(tiles, WIN)
    near_mask = (
        (near_pos[:, None, :] <= query_pos[:, :, None])
        & (near_pos[:, None, :] > query_pos[:, :, None] - WIN)
        & (near_pos[:, None, :] >= 0)
    )[:, None]
    far_mask = (far_pos.reshape(-1)[None, None, :] <= query_pos[:, :, None] - WIN)[:, None]
    return (near_key, near_value, near_score, far_key, far_value, far_score, near_mask, far_mask)


def attention_logits(query_tiles, keys_set, scale):
    near_key, near_value, near_score, far_key, far_value, far_score, near_mask, far_mask = keys_set
    near_raw = jnp.einsum(
        "tqhd,tkhd->thqk", query_tiles, near_key, preferred_element_type=jnp.float32
    )
    far_raw = jnp.einsum("tqhd,khd->thqk", query_tiles, far_key, preferred_element_type=jnp.float32)
    near_gate = jnp.transpose(jax.nn.log_sigmoid(near_score), (0, 2, 1))[:, :, None, :]
    far_gate = jnp.transpose(jax.nn.log_sigmoid(far_score))[None, :, None, :]
    near_logit = jnp.where(near_mask, near_raw * scale + near_gate, very_low)
    far_logit = jnp.where(far_mask, far_raw * scale + far_gate, very_low)
    return (near_logit, far_logit)


def attention_back(query_tiles, keys_set, grad_mixed, log_total, scale):
    near_key, near_value, near_score, far_key, far_value, far_score, near_mask, far_mask = keys_set
    near_logit, far_logit = attention_logits(query_tiles, keys_set, scale)
    near_prob = jnp.exp(near_logit - log_total[..., None])
    far_prob = jnp.exp(far_logit - log_total[..., None])
    near_low = near_prob.astype(jnp.bfloat16)
    far_low = far_prob.astype(jnp.bfloat16)
    grad_near_prob = jnp.einsum(
        "tqhd,tkhd->thqk", grad_mixed, near_value, preferred_element_type=jnp.float32
    )
    grad_far_prob = jnp.einsum(
        "tqhd,khd->thqk", grad_mixed, far_value, preferred_element_type=jnp.float32
    )
    delta = jnp.sum(near_prob * grad_near_prob, axis=-1) + jnp.sum(
        far_prob * grad_far_prob, axis=-1
    )
    grad_near_logit = near_prob * (grad_near_prob - delta[..., None])
    grad_far_logit = far_prob * (grad_far_prob - delta[..., None])
    near_raw_low = (grad_near_logit * scale).astype(jnp.bfloat16)
    far_raw_low = (grad_far_logit * scale).astype(jnp.bfloat16)
    grad_query = jnp.einsum(
        "thqk,tkhd->tqhd", near_raw_low, near_key, preferred_element_type=jnp.float32
    )
    grad_query = grad_query + jnp.einsum(
        "thqk,khd->tqhd", far_raw_low, far_key, preferred_element_type=jnp.float32
    )
    grad_near_key = jnp.einsum(
        "thqk,tqhd->tkhd", near_raw_low, query_tiles, preferred_element_type=jnp.float32
    )
    grad_near_value = jnp.einsum(
        "thqk,tqhd->tkhd", near_low, grad_mixed, preferred_element_type=jnp.float32
    )
    grad_near_score = jnp.transpose(jnp.sum(grad_near_logit, axis=2), (0, 2, 1)) * jax.nn.sigmoid(
        -near_score
    )
    grad_far_key = jnp.einsum(
        "thqk,tqhd->khd", far_raw_low, query_tiles, preferred_element_type=jnp.float32
    )
    grad_far_value = jnp.einsum(
        "thqk,tqhd->khd", far_low, grad_mixed, preferred_element_type=jnp.float32
    )
    grad_far_score = jnp.transpose(jnp.sum(grad_far_logit, axis=(0, 2))) * jax.nn.sigmoid(
        -far_score
    )
    tiles = grad_near_key.shape[0]
    span = grad_near_key.shape[1]
    near_pack = jnp.concatenate(
        [
            grad_near_key.reshape(tiles, span, -1),
            grad_near_value.reshape(tiles, span, -1),
            grad_near_score,
        ],
        axis=-1,
    )
    slots = grad_far_key.shape[0]
    far_pack = jnp.concatenate(
        [grad_far_key.reshape(slots, -1), grad_far_value.reshape(slots, -1), grad_far_score],
        axis=-1,
    )
    return (grad_query, near_pack, far_pack)


def per_device(
    tokens,
    cotangent,
    first_gain,
    first_shift,
    joint_weight,
    query_bias,
    value_bias,
    score_weight,
    out_weight,
    out_bias,
    second_gain,
    second_shift,
    expand_weight,
    expand_bias,
    reduce_weight,
    reduce_bias,
    picks,
    quota,
):
    rows = tokens.shape[1]
    width = tokens.shape[2]
    heads = score_weight.shape[1]
    head_size = width // heads
    tiles = rows // WIN
    blocks = lax.axis_size("seq")
    place = lax.axis_index("seq")
    scale = 1.0 / math.sqrt(head_size)
    inputs = tokens[0].astype(jnp.float32)
    normed, unit_one, inverse_one = layer_norm_parts(inputs, first_gain, first_shift)
    normed_low = normed.astype(jnp.bfloat16)
    joint = jnp.dot(normed_low, joint_weight, preferred_element_type=jnp.float32)
    query = (joint[:, :width] + query_bias).astype(jnp.bfloat16)
    keys = joint[:, width : 2 * width].astype(jnp.bfloat16)
    values = (joint[:, 2 * width :] + value_bias).astype(jnp.bfloat16)
    score = jnp.dot(normed_low, score_weight, preferred_element_type=jnp.float32).astype(
        jnp.bfloat16
    )
    packed = jnp.concatenate([keys, values, score], axis=1)
    channels = packed.shape[1]
    pick_rows = picks[0, 0]
    flat_rows = pick_rows.reshape(-1)
    live = jnp.arange(PICK, dtype=jnp.int32)[None, :] < quota[0, 0][:, None]
    positions = jnp.where(live, place * rows + pick_rows, 2 * rows * blocks)
    sent = packed[flat_rows].reshape(blocks, PICK, channels)
    rim = passed_along(packed[rows - WIN :], "seq", 1)
    far_packed, far_pos = (
        lax.all_to_all(sent, "seq", split_axis=0, concat_axis=0, tiled=True),
        lax.all_to_all(positions, "seq", split_axis=0, concat_axis=0, tiled=True),
    )
    keys_set = arrange(rim, packed, far_packed, far_pos, place, heads, head_size)
    query_tiles = query.reshape(tiles, WIN, heads, head_size)
    near_logit, far_logit = attention_logits(query_tiles, keys_set, scale)
    top = jnp.maximum(jnp.max(near_logit, axis=-1), jnp.max(far_logit, axis=-1))
    total = jnp.sum(jnp.exp(near_logit - top[..., None]), axis=-1) + jnp.sum(
        jnp.exp(far_logit - top[..., None]), axis=-1
    )
    log_total = top + jnp.log(total)
    near_low = jnp.exp(near_logit - log_total[..., None]).astype(jnp.bfloat16)
    far_low = jnp.exp(far_logit - log_total[..., None]).astype(jnp.bfloat16)
    mixed = jnp.einsum("thqk,tkhd->tqhd", near_low, keys_set[1], preferred_element_type=jnp.float32)
    mixed = mixed + jnp.einsum(
        "thqk,khd->tqhd", far_low, keys_set[4], preferred_element_type=jnp.float32
    )
    mixed_low = mixed.reshape(rows, width).astype(jnp.bfloat16)
    attn = jnp.dot(mixed_low, out_weight, preferred_element_type=jnp.float32) + out_bias
    resid = inputs + attn
    normed_two, unit_two, inverse_two = layer_norm_parts(resid, second_gain, second_shift)
    normed_two_low = normed_two.astype(jnp.bfloat16)
    pre = jnp.dot(normed_two_low, expand_weight, preferred_element_type=jnp.float32) + expand_bias
    activated, gelu_pull = jax.vjp(gelu_tanh, pre)
    hidden_low = activated.astype(jnp.bfloat16)
    layer_out = (
        resid + jnp.dot(hidden_low, reduce_weight, preferred_element_type=jnp.float32) + reduce_bias
    ).astype(jnp.bfloat16)
    grad_out_low = cotangent[0]
    grad_out = grad_out_low.astype(jnp.float32)
    reduce_bias_grad = jnp.sum(grad_out, axis=0)
    grad_hidden = times_transposed(grad_out_low, reduce_weight)
    grad_pre_low = gelu_pull(grad_hidden)[0].astype(jnp.bfloat16)
    expand_bias_grad = jnp.sum(grad_pre_low.astype(jnp.float32), axis=0)
    grad_normed_two = times_transposed(grad_pre_low, expand_weight)
    grad_resid_norm, second_gain_grad, second_shift_grad = layer_norm_back(
        grad_normed_two, unit_two, inverse_two, second_gain
    )
    grad_resid = grad_out + grad_resid_norm
    grad_attn_low = grad_resid.astype(jnp.bfloat16)
    out_bias_grad = jnp.sum(grad_attn_low.astype(jnp.float32), axis=0)
    grad_mixed_low = (
        times_transposed(grad_attn_low, out_weight)
        .astype(jnp.bfloat16)
        .reshape(tiles, WIN, heads, head_size)
    )
    rim_back_set = passed_along(packed[rows - WIN :], "seq", 1)
    far_again, pos_again = (
        lax.all_to_all(sent, "seq", split_axis=0, concat_axis=0, tiled=True),
        lax.all_to_all(positions, "seq", split_axis=0, concat_axis=0, tiled=True),
    )
    keys_back = arrange(rim_back_set, packed, far_again, pos_again, place, heads, head_size)
    grad_query, near_pack, far_pack = attention_back(
        query_tiles, keys_back, grad_mixed_low, log_total, scale
    )
    grad_query_low = grad_query.reshape(rows, width).astype(jnp.bfloat16)
    zero_tile = jnp.zeros((1, WIN, channels), jnp.float32)
    extended = jnp.concatenate([near_pack[:, :WIN], zero_tile], axis=0) + jnp.concatenate(
        [zero_tile, near_pack[:, WIN:]], axis=0
    )
    rim_grad = extended[0]
    own_grad = extended[1:].reshape(rows, channels)
    far_grad_low = far_pack.astype(jnp.bfloat16).reshape(blocks, PICK, channels)
    back_far = lax.all_to_all(far_grad_low, "seq", split_axis=0, concat_axis=0, tiled=True)
    back_rim = passed_along(rim_grad.astype(jnp.bfloat16), "seq", -1)
    own_total = own_grad + jnp.concatenate(
        [jnp.zeros((rows - WIN, channels), jnp.float32), back_rim.astype(jnp.float32)], axis=0
    )
    own_total = own_total.at[flat_rows].add(
        back_far.reshape(blocks * PICK, channels).astype(jnp.float32)
    )
    grad_packed_low = own_total.astype(jnp.bfloat16)
    grad_key_low = grad_packed_low[:, :width]
    grad_value_low = grad_packed_low[:, width : 2 * width]
    grad_score_low = grad_packed_low[:, 2 * width :]
    grad_joint_low = jnp.concatenate([grad_query_low, grad_key_low, grad_value_low], axis=1)
    query_bias_grad = jnp.sum(grad_query_low.astype(jnp.float32), axis=0)
    value_bias_grad = jnp.sum(grad_value_low.astype(jnp.float32), axis=0)
    score_weight_grad = cross(normed_low, grad_score_low)
    grad_normed = times_transposed(grad_joint_low, joint_weight) + times_transposed(
        grad_score_low, score_weight
    )
    grad_input_norm, first_gain_grad, first_shift_grad = layer_norm_back(
        grad_normed, unit_one, inverse_one, first_gain
    )
    token_grad = (grad_resid + grad_input_norm)[None]
    joint_weight_grad = cross(normed_low, grad_joint_low)
    out_weight_grad = cross(mixed_low, grad_attn_low)
    expand_weight_grad = cross(normed_two_low, grad_pre_low)
    reduce_weight_grad = cross(hidden_low, grad_out_low)
    (
        first_gain_grad,
        first_shift_grad,
        joint_weight_grad,
        query_bias_grad,
        value_bias_grad,
        score_weight_grad,
        out_weight_grad,
        out_bias_grad,
        second_gain_grad,
        second_shift_grad,
        expand_weight_grad,
        expand_bias_grad,
        reduce_weight_grad,
        reduce_bias_grad,
    ) = lax.psum(
        (
            first_gain_grad,
            first_shift_grad,
            joint_weight_grad,
            query_bias_grad,
            value_bias_grad,
            score_weight_grad,
            out_weight_grad,
            out_bias_grad,
            second_gain_grad,
            second_shift_grad,
            expand_weight_grad,
            expand_bias_grad,
            reduce_weight_grad,
            reduce_bias_grad,
        ),
        ("dp", "seq"),
    )
    return (
        layer_out[None],
        token_grad,
        first_gain_grad,
        first_shift_grad,
        joint_weight_grad,
        query_bias_grad,
        value_bias_grad,
        score_weight_grad,
        out_weight_grad,
        out_bias_grad,
        second_gain_grad,
        second_shift_grad,
        expand_weight_grad,
        expand_bias_grad,
        reduce_weight_grad,
        reduce_bias_grad,
    )


def solution(mesh):
    placed = (
        P("dp", "seq", None),
        P("dp", "seq", None),
        P(),
        P(),
        P(),
        P(),
        P(),
        P(),
        P(),
        P(),
        P(),
        P(),
        P(),
        P(),
        P(),
        P(),
        P("dp", "seq", None, None),
        P("dp", "seq", None),
    )
    return jax.shard_map(
        per_device,
        mesh=mesh,
        in_specs=placed,
        out_specs=(
            P("dp", "seq", None),
            P("dp", "seq", None),
            P(),
            P(),
            P(),
            P(),
            P(),
            P(),
            P(),
            P(),
            P(),
            P(),
            P(),
            P(),
            P(),
            P(),
        ),
        check_vma=False,
    )
```

profile of v0, /device:TPU:0, one launch (start us, length us, event | category | flops | bytes accessed | tf_op | source)
XLA Modules:
  0.0 999.5 jit_solution(8566734394154111945)
XLA Ops:
  58.0 9.3 copy.263
  83.5 7.7 fusion.147
  98.5 9.3 copy.262
  116.2 6.9 fusion.148
  152.4 8.4 fusion.143
  160.8 10.7 %fusion.73 = f32[3072,768]{1,0:T(8,128)} fusion(bf16[1,1024,768]{2,1,0:T(8,128)(2,1)S(1)} %copy-done.30, f32[1024,3072]{1,0:T(8,128)S(1)} %fusion.143, f32[3072]{0:T(1024)S(1)} %copy-done.62), kind=kOutput, calls=%fused_computation.117 | convolution fusion | flops 4863295488 | bytes 23605248 | tf_op jit(solution)/shard_map/dot_general | solution.py:45
  171.6 18.3 %convert_reduce_fusion = (f32[3072]{0:T(1024)}, bf16[1024,3072]{1,0:T(8,128)(2,1)}) fusion(bf16[3072,768]{1,0:T(8,128)(2,1)} %param.32, bf16[1,1024,768]{2,1,0:T(8,128)(2,1)} %param.19, f32[1024,3072]{1,0:T(8,128)S(1)} %fusion.143, f32[3072]{0:T(1024)S(1)} %copy-done.62), kind=kOutput, calls=%fused_computation.13 | convolution fusion | flops 4916769792 | bytes 25190400 | tf_op jit(solution)/shard_map/dot_general | solution.py:51
  189.9 10.5 %fusion.150 = (f32[768]{0:T(1024)}, f32[1024,768]{1,0:T(8,128)}) fusion(bf16[1024,3072]{1,0:T(8,128)(2,1)} %get-tuple-element.170, bf16[768,3072]{1,0:T(8,128)(2,1)} %param.30), kind=kOutput, calls=%fused_computation.212 | convolution fusion | flops 4832623616 | bytes 14158848 | tf_op jit(solution)/shard_map/dot_general | solution.py:51
  200.3 7.9 fusion.142
  239.6 9.2 multiply_reduce_fusion
  271.0 9.7 multiply_convert_fusion.2
  283.7 7.4 fusion.54
  291.1 6.5 copy.297
  297.6 9.9 pad_maximum_fusion
  307.5 11.4 %fusion.144 = (f32[16,64,1548]{2,1,0:T(8,128)}, f32[16,64,1548]{2,1,0:T(8,128)}) fusion(f32[16,128,1548]{2,1,0:T(8,128)} %pad_maximum_fusion), kind=kLoop, calls=%fused_computation.206 | loop fusion | bytes 25362432 | tf_op jit(solution)/shard_map/slice | solution.py:266
  343.4 8.6 convert_reduce_fusion.1
  371.3 7.4 scatter_custom_fusion
  386.6 6.9 fusion.28
  393.6 9.6 fusion.38
  403.2 12.0 %fusion.78 = bf16[1,1024,768]{1,2,0:T(8,128)(2,1)} fusion(f32[768]{0:T(1024)} %param.33, f32[1024,768]{0,1:T(8,128)} %copy-done.6, bf16[3072,768]{1,0:T(8,128)(2,1)} %param.32, f32[1024,3072]{1,0:T(8,128)} %copy-done.18, f32[3072]{0:T(1024)} %param.31), kind=kOutput, calls=%fused_computation.122 | convolution fusion | flops 4865654784 | bytes 22035456 | tf_op jit(solution)/shard_map/dot_general | solution.py:234
  428.0 94.7 %all-reduce.8.cloned.1.call-done = (f32[768]{0:T(1024)}, f32[768]{0:T(1024)}, f32[768]{0:T(1024)}, f32[768]{0:T(1024)}, f32[768,12]{0,1:T(8,128)}, /*index=5*/f3...) async-done(((f32[768]{0:T(1024)}, f32[768]{0:T(1024)}, f32[768]{0:T(1024)}, f32[768]{0:T(1024)}, f32[768,12]{0,1:T(8,128)}, ...) | async-done | bytes 73744 | tf_op jit(solution)/shard_map/psum | solution.py:313
  522.7 441.9 %all-reduce.10.cloned.1.call-done = (f32[768,2304]{1,0:T(8,128)}, f32[768,768]{1,0:T(8,128)}, f32[768,3072]{1,0:T(8,128)}, f32[3072,768]{1,0:T(8,128)}) async-done(((f32[768,2304]{1,0:T(8,128)}, f32[768,768]{1,0:T(8,128)}, f32[768,3072]{1,0:T(8,128)}, f32[3072,768]{1,0:T(8,128)}), (f32[768,2304]{1,0:T(8,128)}, f32[768,768]{1,0:T(8,128)}, f32[768,3072]{1,0:T(8,128)}, ...) | async-done | bytes 28311568 | tf_op jit(solution)/shard_map/psum | solution.py:313
  967.1 6.6 copy.431
  978.7 8.8 copy.439
  (275 shorter events, 244.9 us)
Async XLA Ops:
  7.2 17.4 %copy-start = (bf16[768,2304]{1,0:T(8,128)(2,1)S(1)}, bf16[768,2304]{1,0:T(8,128)(2,1)}, u32[]{:S(2)}) copy-start(bf16[768,2304]{1,0:T(8,128)(2,1)} %param.22) | copy-start | bytes 10616836
  7.2 13.0 %copy-start.47 = (f32[768]{0:T(1024)S(1)}, f32[768]{0:T(1024)}, u32[]{:S(2)}) copy-start(f32[768]{0:T(1024)} %param.20) | copy-start | bytes 9220
  7.2 13.0 %copy-start.51 = (f32[768]{0:T(1024)S(1)}, f32[768]{0:T(1024)}, u32[]{:S(2)}) copy-start(f32[768]{0:T(1024)} %param.21) | copy-start | bytes 9220
  8.7 58.6 %all-to-all-start = ((s32[8,1,8]{2,1,0:T(1,128)}), s32[8,1,8]{2,1,0:T(1,128)}, u32[]{:S(2)}, u32[]{:S(2)}) async-start(s32[8,1,8]{2,1,0:T(1,128)} %bitcast.8), calls=%async_computation | async-start | bytes 8192 | tf_op jit(solution)/shard_map/all_to_all | solution.py:209
  35.6 57.3 %collective-permute-start = (bf16[64,1548]{1,0:T(8,128)(2,1)}, bf16[64,1548]{1,0:T(8,128)(2,1)}, u32[]{:S(2)}, u32[]{:S(2)}) collective-permute-start(bf16[64,1548]{1,0:T(8,128)(2,1)} %slice.111), channel_id=1, source_target_pairs={{0,1},{1,2},{2,3},{3,4},{4,5},{5,6},{6,7},{8,9},{9,10},{10,11},{11... | collective-permute-start | bytes 594440 | tf_op jit(solution)/shard_map/ppermute | solution.py:16
  67.3 10.6 %all-to-all-start.1 = ((bf16[8,8,1548]{2,1,0:T(8,128)(2,1)}), bf16[8,8,1548]{2,1,0:T(8,128)(2,1)}, u32[]{:S(2)}, u32[]{:S(2)}) async-start(bf16[8,8,1548]{2,1,0:T(8,128)(2,1)} %bitcast.194), calls=%async_computation.1 | async-start | bytes 425984 | tf_op jit(solution)/shard_map/all_to_all | solution.py:208
  116.1 16.9 %copy-start.10 = (bf16[16,128,768]{1,0,2:T(8,128)(2,1)}, bf16[16,128,768]{1,0,2:T(8,128)(2,1)S(1)}, u32[]{:S(2)}) copy-start(bf16[16,128,768]{1,0,2:T(8,128)(2,1)S(1)} %get-tuple-element.145) | copy-start | bytes 9437188
  123.1 9.9 copy-start.1
  151.9 48.4 %copy-start.6 = (f32[1024,768]{0,1:T(8,128)}, f32[1024,768]{0,1:T(8,128)S(1)}, u32[]{:S(2)}) copy-start(f32[1024,768]{0,1:T(8,128)S(1)} %get-tuple-element.159) | copy-start | bytes 9437188
  160.8 10.7 %copy-start.18 = (f32[1024,3072]{1,0:T(8,128)}, f32[1024,3072]{1,0:T(8,128)S(1)}, u32[]{:S(2)}) copy-start(f32[1024,3072]{1,0:T(8,128)S(1)} %fusion.143) | copy-start | bytes 37748740
  189.9 10.5 %copy-start.64 = (bf16[1024,3072]{1,0:T(8,128)(2,1)S(1)}, bf16[1024,3072]{1,0:T(8,128)(2,1)}, u32[]{:S(2)}) copy-start(bf16[1024,3072]{1,0:T(8,128)(2,1)} %get-tuple-element.170) | copy-start | bytes 18874372
  233.8 15.0 %slice-start.4 = ((s8[6291456]{0:T(1024)(128)(4,1)}), s8[4194304]{0:T(1024)(128)(4,1)S(1)}, s32[]{:S(2)}) async-start(s8[6291456]{0:T(1024)(128)(4,1)} %bitcast.180), calls=%async_computation.9 | async-start | bytes 8388608
  233.8 19.6 %slice-start.2 = ((s8[6291456]{0:T(1024)(128)(4,1)}), s8[4194304]{0:T(1024)(128)(4,1)S(1)}, s32[]{:S(2)}) async-start(s8[6291456]{0:T(1024)(128)(4,1)} %bitcast.178), calls=%async_computation.7 | async-start | bytes 8388608
  239.6 9.2 slice-start.5
  239.6 9.2 copy-start.2
  239.6 13.8 %slice-start.3 = ((s8[6291456]{0:T(1024)(128)(4,1)}), s8[2097152]{0:T(1024)(128)(4,1)S(1)}, s32[]{:S(2)}) async-start(s8[6291456]{0:T(1024)(128)(4,1)} %bitcast.178), calls=%async_computation.8 | async-start | bytes 4194304
  271.0 9.7 copy-start.36
  338.0 33.4 %all-to-all-start.2 = ((bf16[8,8,1548]{2,1,0:T(8,128)(2,1)}), bf16[8,8,1548]{2,1,0:T(8,128)(2,1)}, u32[]{:S(2)}, u32[]{:S(2)}) async-start(bf16[8,8,1548]{2,1,0:T(8,128)(2,1)} %pad_maximum_fusion.10), calls=%async_computation.2 | async-start | bytes 425984 | tf_op jit(solution)/shard_map/all_to_all | solution.py:271
  342.0 180.7 %all-reduce.8.cloned.1.call-start = ((), (), s32[]{:S(2)}) async-start(), calls=%async_computation.3 | async-start | bytes 188416 | tf_op jit(solution)/shard_map/psum | solution.py:313
  342.1 23.1 %collective-permute-start.1 = (bf16[64,1548]{1,0:T(8,128)(2,1)}, bf16[64,1548]{1,0:T(8,128)(2,1)}, u32[]{:S(2)}, u32[]{:S(2)}) collective-permute-start(bf16[64,1548]{1,0:T(8,128)(2,1)} %fusion.106), channel_id=1, source_target_pairs={{1,0},{2,1},{3,2},{4,3},{5,4},{6,5},{7,6},{9,8},{10,9},{11,10},{12... | collective-permute-start | bytes 594440 | tf_op jit(solution)/shard_map/ppermute | solution.py:16
  393.5 571.0 %all-reduce.10.cloned.1.call-start = ((), (), s32[]{:S(2)}) async-start(), calls=%async_computation.4 | async-start | bytes 56623104 | tf_op jit(solution)/shard_map/psum | solution.py:313
  975.5 12.6 %slice-start.6 = ((s8[9437184]{0:T(1024)(128)(4,1)}), s8[4194304]{0:T(1024)(128)(4,1)S(1)}, s32[]{:S(2)}) async-start(s8[9437184]{0:T(1024)(128)(4,1)} %bitcast.190), calls=%async_computation.11 | async-start | bytes 8388608
  978.7 9.4 slice-start.7
  978.7 9.4 slice-start.8
  (57 other events, 250.0 us)
Sparse Core Ops, SparseCore 0:
  393.6 129.0 all-reduce.7
  531.4 433.1 all-reduce.9
where the time goes:
time: 1010 us; the launch traced here: 999 us
  waiting for transfers between devices  540 us (53%)
  matrix products  169 us (17%)
  local copies, waits for them, and re-layouts  161 us (16%)
  other arithmetic  96.7 us (10%)
  starting transfers between devices  17.9 us (2%)
  between operations  15 us (1%)
    psum x2, waiting for transfers between devices, per_device(): lax.psum((first_gain_grad, first_shift_grad, joint_weight_grad, query_bia...  537 us
    unnamed x167, local copies, waits for them, and re-layouts  50.3 us
    dot_general x5, matrix products, times_transposed(): lax.dot_general(left, right, (((1,), (1,)), ((), ())), preferred_element_...  38.9 us
    dot_general x5, matrix products, cross(): lax.dot_general(left, right, (((0,), (0,)), ((), ())), preferred_element_...  32.2 us
  transfers between devices with their start and end apart: 7, of which 3 were waited for; matrix products, arithmetic and copies ran while one was open for 13% of the time, Pallas kernels for 0%

commit v1 on v0

--- a/solution.py
+++ b/solution.py
@@ -311,23 +311,26 @@
         reduce_weight_grad,
         reduce_bias_grad,
     ) = lax.psum(
-        (
-            first_gain_grad,
-            first_shift_grad,
-            joint_weight_grad,
-            query_bias_grad,
-            value_bias_grad,
-            score_weight_grad,
-            out_weight_grad,
-            out_bias_grad,
-            second_gain_grad,
-            second_shift_grad,
-            expand_weight_grad,
-            expand_bias_grad,
-            reduce_weight_grad,
-            reduce_bias_grad,
+        lax.psum(
+            (
+                first_gain_grad,
+                first_shift_grad,
+                joint_weight_grad,
+                query_bias_grad,
+                value_bias_grad,
+                score_weight_grad,
+                out_weight_grad,
+                out_bias_grad,
+                second_gain_grad,
+                second_shift_grad,
+                expand_weight_grad,
+                expand_bias_grad,
+                reduce_weight_grad,
+                reduce_bias_grad,
+            ),
+            "seq",
         ),
-        ("dp", "seq"),
+        "dp",
     )
     return (
         layer_out[None],

time: 1010 us -> 1830 us (1.81)
  waiting for transfers between devices: 540 us -> 1360 us
    psum x0 -> x2, waiting for transfers between devices: none -> 955 us  [per_device(): lax.psum(lax.psum((first_gain_grad, first_shift_grad, joint_weight_grad,...]
    psum x2, waiting for transfers between devices: 537 us -> 398 us  [per_device(): lax.psum((first_gain_grad, first_shift_grad, joint_weight_grad, query_bia...]
  transfers between devices with their start and end apart: 7 -> 9, of which waited for: 3 -> 5; matrix products, arithmetic and copies ran while one was open for 13% -> 7% of each run, Pallas kernels for 0% -> 0%
where the time goes in v1:
time: 1830 us; the launch traced here: 1820 us
  waiting for transfers between devices  1360 us (74%)
  matrix products  169 us (9%)
  local copies, waits for them, and re-layouts  161 us (9%)
  other arithmetic  96.6 us (5%)
    psum x2, waiting for transfers between devices, per_device(): lax.psum(lax.psum((first_gain_grad, first_shift_grad, joint_weight_grad,...  955 us
    psum x2, waiting for transfers between devices, per_device(): lax.psum((first_gain_grad, first_shift_grad, joint_weight_grad, query_bia...  398 us
    unnamed x167, local copies, waits for them, and re-layouts  50.3 us
    dot_general x5, matrix products, times_transposed(): lax.dot_general(left, right, (((1,), (1,)), ((), ())), preferred_element_...  38.9 us
  transfers between devices with their start and end apart: 9, of which 5 were waited for; matrix products, arithmetic and copies ran while one was open for 7% of the time, Pallas kernels for 0%

profile of v1, /device:TPU:0, one launch (start us, length us, event | category | flops | bytes accessed | tf_op | source)
XLA Modules:
  0.0 1815.5 jit_solution(13978368618682900913)
XLA Ops:
  58.0 9.3 copy.263
  83.4 7.7 fusion.147
  98.4 9.3 copy.262
  116.1 6.9 fusion.148
  152.3 8.4 fusion.143
  160.7 10.7 fusion.73
  171.4 18.3 %convert_reduce_fusion = (f32[3072]{0:T(1024)}, bf16[1024,3072]{1,0:T(8,128)(2,1)}) fusion(bf16[3072,768]{1,0:T(8,128)(2,1)} %param.32, bf16[1,1024,768]{2,1,0:T(8,128)(2,1)} %param.19, f32[1024,3072]{1,0:T(8,128)S(1)} %fusion.143, f32[3072]{0:T(1024)S(1)} %copy-done.62), kind=kOutput, calls=%fused_computation.13 | convolution fusion | flops 4916769792 | bytes 25190400 | tf_op jit(solution)/shard_map/dot_general | solution.py:51
  189.7 10.5 fusion.150
  200.2 7.9 fusion.142
  239.4 9.2 multiply_reduce_fusion
  270.8 9.7 multiply_convert_fusion.2
  283.5 7.4 fusion.54
  297.4 9.9 pad_maximum_fusion
  307.3 11.5 fusion.144
  343.2 8.6 convert_reduce_fusion.1
  371.2 7.4 scatter_custom_fusion
  386.4 6.9 fusion.28
  393.4 9.6 fusion.38
  403.1 48.0 %all-reduce.12.cloned.1.call-done = (f32[768]{0:T(1024)}, f32[768]{0:T(1024)}, f32[768]{0:T(1024)}, f32[768]{0:T(1024)}, f32[768,12]{0,1:T(8,128)}, /*index=5*/f...) async-done(((f32[768]{0:T(1024)}, f32[768]{0:T(1024)}, f32[768]{0:T(1024)}, f32[768]{0:T(1024)}, f32[768,12]{0,1:T(8,128)}, ...) | async-done | bytes 73744 | tf_op jit(solution)/shard_map/psum | solution.py:314
  451.2 349.7 %all-reduce.14.cloned.1.call-done = (f32[768,2304]{1,0:T(8,128)}, f32[768,768]{1,0:T(8,128)}, f32[768,3072]{1,0:T(8,128)}, f32[3072,768]{1,0:T(8,128)}) async-done(((f32[768,2304]{1,0:T(8,128)}, f32[768,768]{1,0:T(8,128)}, f32[768,3072]{1,0:T(8,128)}, f32[3072,768]{1,0:T(8,128)}), (f32[768,2304]{1,0:T(8,128)}, f32[768,768]{1,0:T(8,128)}, f32[768,3072]{1,0:T(8,128)}, ...) | async-done | bytes 28311568 | tf_op jit(solution)/shard_map/psum | solution.py:314
  800.9 11.9 fusion.78
  825.6 14.4 all-reduce.16.cloned.1.call-done
  840.0 940.9 %all-reduce.18.cloned.1.call-done = (f32[768,2304]{1,0:T(8,128)}, f32[768,768]{1,0:T(8,128)}, f32[768,3072]{1,0:T(8,128)}, f32[3072,768]{1,0:T(8,128)}) async-done(((f32[768,2304]{1,0:T(8,128)}, f32[768,768]{1,0:T(8,128)}, f32[768,3072]{1,0:T(8,128)}, f32[3072,768]{1,0:T(8,128)}), (f32[768,2304]{1,0:T(8,128)}, f32[768,768]{1,0:T(8,128)}, f32[768,3072]{1,0:T(8,128)}, ...) | async-done | bytes 28311568 | tf_op jit(solution)/shard_map/psum | solution.py:313
  1795.0 8.8 copy.453
  (281 shorter events, 258.0 us)
Async XLA Ops:
  7.2 17.4 copy-start
  7.2 13.0 copy-start.47
  7.2 13.0 copy-start.51
  8.7 58.5 %all-to-all-start = ((s32[8,1,8]{2,1,0:T(1,128)}), s32[8,1,8]{2,1,0:T(1,128)}, u32[]{:S(2)}, u32[]{:S(2)}) async-start(s32[8,1,8]{2,1,0:T(1,128)} %bitcast.8), calls=%async_computation | async-start | bytes 8192 | tf_op jit(solution)/shard_map/all_to_all | solution.py:209
  35.6 57.2 %collective-permute-start = (bf16[64,1548]{1,0:T(8,128)(2,1)}, bf16[64,1548]{1,0:T(8,128)(2,1)}, u32[]{:S(2)}, u32[]{:S(2)}) collective-permute-start(bf16[64,1548]{1,0:T(8,128)(2,1)} %slice.111), channel_id=1, source_target_pairs={{0,1},{1,2},{2,3},{3,4},{4,5},{5,6},{6,7},{8,9},{9,10},{10,11},{11... | collective-permute-start | bytes 594440 | tf_op jit(solution)/shard_map/ppermute | solution.py:16
  67.3 10.6 all-to-all-start.1
  116.0 16.9 copy-start.10
  123.0 9.9 copy-start.1
  151.8 48.4 %copy-start.6 = (f32[1024,768]{0,1:T(8,128)}, f32[1024,768]{0,1:T(8,128)S(1)}, u32[]{:S(2)}) copy-start(f32[1024,768]{0,1:T(8,128)S(1)} %get-tuple-element.173) | copy-start | bytes 9437188
  160.7 10.7 copy-start.18
  189.7 10.5 copy-start.64
  233.6 15.0 slice-start.4
  233.6 19.4 %slice-start.2 = ((s8[6291456]{0:T(1024)(128)(4,1)}), s8[4194304]{0:T(1024)(128)(4,1)S(1)}, s32[]{:S(2)}) async-start(s8[6291456]{0:T(1024)(128)(4,1)} %bitcast.178), calls=%async_computation.9 | async-start | bytes 8388608
  239.4 13.6 slice-start.3
  270.8 9.7 copy-start.36
  337.8 33.4 %all-to-all-start.2 = ((bf16[8,8,1548]{2,1,0:T(8,128)(2,1)}), bf16[8,8,1548]{2,1,0:T(8,128)(2,1)}, u32[]{:S(2)}, u32[]{:S(2)}) async-start(bf16[8,8,1548]{2,1,0:T(8,128)(2,1)} %pad_maximum_fusion.10), calls=%async_computation.2 | async-start | bytes 425984 | tf_op jit(solution)/shard_map/all_to_all | solution.py:271
  341.8 109.3 %all-reduce.12.cloned.1.call-start = ((), (), s32[]{:S(2)}) async-start(), calls=%async_computation.3 | async-start | bytes 188416 | tf_op jit(solution)/shard_map/psum | solution.py:314
  341.9 23.1 %collective-permute-start.1 = (bf16[64,1548]{1,0:T(8,128)(2,1)}, bf16[64,1548]{1,0:T(8,128)(2,1)}, u32[]{:S(2)}, u32[]{:S(2)}) collective-permute-start(bf16[64,1548]{1,0:T(8,128)(2,1)} %fusion.106), channel_id=1, source_target_pairs={{1,0},{2,1},{3,2},{4,3},{5,4},{6,5},{7,6},{9,8},{10,9},{11,10},{12... | collective-permute-start | bytes 594440 | tf_op jit(solution)/shard_map/ppermute | solution.py:16
  393.4 407.5 %all-reduce.14.cloned.1.call-start = ((), (), s32[]{:S(2)}) async-start(), calls=%async_computation.4 | async-start | bytes 56623104 | tf_op jit(solution)/shard_map/psum | solution.py:314
  403.1 437.0 %all-reduce.16.cloned.1.call-start = ((), (), s32[]{:S(2)}) async-start(), calls=%async_computation.5 | async-start | bytes 188416 | tf_op jit(solution)/shard_map/psum | solution.py:313
  451.2 1329.7 %all-reduce.18.cloned.1.call-start = ((), (), s32[]{:S(2)}) async-start(), calls=%async_computation.6 | async-start | bytes 56623104 | tf_op jit(solution)/shard_map/psum | solution.py:313
  1791.8 12.6 slice-start.6
  1795.0 9.4 slice-start.7
  1795.0 9.4 slice-start.8
  (59 other events, 268.1 us)
Sparse Core Ops, SparseCore 0:
  393.5 57.6 all-reduce.11
  457.2 343.6 all-reduce.13
  804.4 35.5 all-reduce.15
  842.8 938.0 all-reduce.17
